TPU v7x, 256 devices: a whole 4x4x8 slice. The times are simulated.
256 devices in a mesh: grp: 1, blk: 32 (over y, x, core), head: 8 (over z).
Axes of the slice: x: 4, y: 4, z: 8, core: 2. Of those that a mesh axis runs over, the one named last changes fastest.
Arguments:
- answer_probe_vectors: bfloat16 [32, 128, 8192], P(('grp', 'blk'), None, 'head')
- answer_lookup_vectors: bfloat16 [32, 128, 1024], P(('grp', 'blk'), None, 'head'), may hold values from -6 to 6
- answer_content_vectors: bfloat16 [32, 128, 1024], P(('grp', 'blk'), None, 'head'), may hold values from -6 to 6
- common_context_lookups: bfloat16 [16384, 1024], P(('grp', 'blk'), 'head')
- common_context_contents: bfloat16 [16384, 1024], P(('grp', 'blk'), 'head'), may hold values from -6 to 6
- place_answer_number: int32 [32], P('grp'), may hold values from 0 to 31, each once
- answer_token_count: int32 [32], P(('grp', 'blk')), may hold values from 32 to 128, as said below
- passing_answers: int32 [1], P('grp'), may hold values from 8 to 32
Outputs:
- attended: bfloat16 [32, 128, 8192], P(('grp', 'blk'), None, 'head')
Inputs may be any that keep to these rules, and one draw needn't show every extreme that they name: `place_answer_number`: each response of the group stands in exactly one slot. `answer_token_count`: some slot holds a response of 128 tokens, some one of 32.
All inputs are finite; a program needn't handle non-finite values.
Results may differ from a plain program's by a relative error of at most 0.01.
Values may be sent and summed in bfloat16 or wider, within the bound.
No kernel may reach another device: no remote copies, remote signals or barrier semaphores. Data moves between devices by JAX's collectives and lax.ppermute only.
A program may use at most 192 MiB of HBM per device.

v0:
```python
import functools

import jax
import jax.numpy as jnp
import numpy as np
from jax import lax
from jax.experimental import pallas as pl
from jax.experimental.pallas import tpu as pltpu
from jax.sharding import PartitionSpec as P

WIDTH = 128
HEADS = 8
TOKENS = 128
PIECE = 512
STEP = 32
SCALE = float(np.log2(np.e) / np.sqrt(WIDTH))
ROWS, COLS = 4, 4
F32, BF16 = jnp.float32, jnp.bfloat16


def place(y, x, c):
    return (y * COLS + x) * 2 + c


def swapped(block, y_bits, x_bits, c_bits):
    route = [
        (place(y, x, c), place(y ^ y_bits, x ^ x_bits, c ^ c_bits))
        for y in range(ROWS)
        for x in range(COLS)
        for c in range(2)
    ]
    return lax.ppermute(block, "blk", route)


def dot_t(a, b):
    return lax.dot_general(a, b, (((1,), (1,)), ((), ())), preferred_element_type=F32)


def dot(a, b):
    return lax.dot_general(a, b, (((1,), (0,)), ((), ())), preferred_element_type=F32)


def lane_max(s):
    best = s[:, :128]
    for j in range(1, s.shape[1] // 128):
        best = jnp.maximum(best, s[:, j * 128 : (j + 1) * 128])
    return jnp.max(best, 1, keepdims=True)


def split_scaled(q):
    full = q.astype(F32) * SCALE
    high = full.astype(BF16)
    low = (full - high.astype(F32)).astype(BF16)
    return jnp.concatenate([high, low], 1)


def twice(k):
    return jnp.concatenate([k, k], 1)


def with_ones(v):
    return jnp.concatenate([v, jnp.ones_like(v)], 1)


def kept_tokens(q_ref):
    return jnp.max(q_ref[TOKENS:, :WIDTH].astype(F32)).astype(jnp.int32)


def rows_of(q_ref, row, tokens):
    return jnp.concatenate(
        [q_ref[pl.ds(row, tokens), h * WIDTH : (h + 1) * WIDTH] for h in range(HEADS)], 0
    )


def steps_of(q_ref):
    return (kept_tokens(q_ref) + (STEP - 1)) // STEP


def far_kernel(n_kv, q_ref, q_far_ref, *refs):
    kv_refs, own_refs, (o_far_ref, o_own_ref) = refs[:n_kv], refs[n_kv : n_kv + 2], refs[n_kv + 2 :]
    mine, far = steps_of(q_ref), steps_of(q_far_ref)
    slot_over_prompt(q_far_ref, kv_refs, (), o_far_ref, 0, far)
    slot_over_prompt(q_ref, kv_refs, own_refs, o_own_ref, 0, jnp.maximum(mine - far, 0))


def near_kernel(n_kv, q_ref, q_far_ref, q_a_ref, q_b_ref, *refs):
    kv_refs, own_refs, refs = refs[:n_kv], refs[n_kv : n_kv + 2], refs[n_kv + 2 :]
    old_own_ref, o_a_ref, o_b_ref, o_own_ref = refs
    o_own_ref[...] = old_own_ref[...]
    mine, far, near_a, near_b = map(steps_of, (q_ref, q_far_ref, q_a_ref, q_b_ref))
    least = jnp.minimum(jnp.minimum(mine, far), jnp.minimum(near_a, near_b))
    slot_over_prompt(q_a_ref, kv_refs, (), o_a_ref, 0, near_a)
    slot_over_prompt(q_b_ref, kv_refs, (), o_b_ref, 0, near_b)
    slot_over_prompt(q_ref, kv_refs, own_refs, o_own_ref, jnp.maximum(mine - far, 0), mine - least)


def own_kernel(n_kv, q_ref, q_far_ref, q_a_ref, q_b_ref, *refs):
    kv_refs, own_refs, (old_own_ref, o_own_ref) = refs[:n_kv], refs[n_kv : n_kv + 2], refs[n_kv + 2 :]
    o_own_ref[...] = old_own_ref[...]
    mine, far, near_a, near_b = map(steps_of, (q_ref, q_far_ref, q_a_ref, q_b_ref))
    least = jnp.minimum(jnp.minimum(mine, far), jnp.minimum(near_a, near_b))
    slot_over_prompt(q_ref, kv_refs, own_refs, o_own_ref, mine - least, mine)


def slot_over_prompt(q_ref, kv_refs, own_refs, o_ref, begin, end):
    count = kept_tokens(q_ref)

    def block(row, tokens):
        rows = tokens * HEADS
        q = split_scaled(rows_of(q_ref, row, tokens))
        peak = total = None
        if own_refs:
            own_k_ref, own_v_ref = own_refs
            shape = (rows, TOKENS)
            token = row + (lax.broadcasted_iota(jnp.int32, shape, 0) & (tokens - 1))
            u = lax.broadcasted_iota(jnp.int32, shape, 1)
            allowed = (u <= token) & (u < count)
            s = jnp.where(allowed, dot_t(q, twice(own_k_ref[...])), F32(-1e30))
            peak = jnp.max(s, 1, keepdims=True)
            e = jnp.where(allowed, jnp.exp2(s - peak), F32(0.0))
            total = dot(e.astype(BF16), with_ones(own_v_ref[...]))
        parts = [
            (ref, start) for ref in kv_refs for start in range(0, ref.shape[0], 2 * PIECE)
        ]

        def scores(n):
            ref, start = parts[n]
            return dot_t(q, twice(ref[start : start + PIECE, :]))

        following = scores(0)
        for n, (ref, start) in enumerate(parts):
            s = following
            if n + 1 < len(parts):
                following = scores(n + 1)
            top = lane_max(s)
            if peak is not None:
                top = jnp.maximum(peak, top)
            e = jnp.exp2(s - top).astype(BF16)
            added = dot(e, with_ones(ref[start + PIECE : start + 2 * PIECE, :]))
            total = added if peak is None else total * jnp.exp2(peak - top) + added
            peak = top
        lane = lax.broadcasted_iota(jnp.int32, (tokens, WIDTH), 1)
        packed_sum = packed_peak = jnp.zeros((tokens, WIDTH), F32)
        sums = total[:, WIDTH:]
        out = (total[:, :WIDTH] / sums).astype(BF16)
        for h in range(HEADS):
            mine, at = (lane & (HEADS - 1)) == h, slice(h * tokens, (h + 1) * tokens)
            o_ref[pl.ds(row, tokens), h * WIDTH : (h + 1) * WIDTH] = out[at]
            packed_sum = jnp.where(mine, sums[at], packed_sum)
            packed_peak = jnp.where(mine, peak[at], packed_peak)
        lse = packed_peak + jnp.log2(packed_sum)
        high = lse.astype(BF16).astype(F32)
        middle = (lse - high).astype(BF16).astype(F32)
        low = lse - high - middle
        stats = jnp.where(lane < HEADS, high, jnp.where(lane < 2 * HEADS, middle, low))
        o_ref[pl.ds(row, tokens), HEADS * WIDTH :] = stats.astype(BF16)

    def pair(i, carry):
        block(pl.multiple_of((begin + 2 * i) * STEP, STEP), 2 * STEP)
        return carry

    lax.fori_loop(0, (end - begin) // 2, pair, 0)

    @pl.when((end - begin) % 2 == 1)
    def _():
        block(pl.multiple_of((end - 1) * STEP, STEP), STEP)


def merge_kernel(n, q_ref, *refs):
    part_refs, o_ref = refs[:n], refs[n]
    count = kept_tokens(q_ref)
    keep = lax.broadcasted_iota(jnp.int32, (TOKENS, WIDTH), 0) < count
    lses = []
    for ref in part_refs:
        stats = ref[:, HEADS * WIDTH :].astype(F32)
        lses.append(
            stats
            + pltpu.roll(stats, WIDTH - HEADS, 1)
            + pltpu.roll(stats, WIDTH - 2 * HEADS, 1)
        )
    peak = functools.reduce(jnp.maximum, lses)
    weights = [jnp.exp2(v - peak) for v in lses]
    inverse = 1.0 / sum(weights)
    weights = [w * inverse for w in weights]
    for h in range(HEADS):
        cols = slice(h * WIDTH, (h + 1) * WIDTH)
        out = sum(
            ref[:, cols].astype(F32) * w[:, h : h + 1]
            for ref, w in zip(part_refs, weights, strict=True)
        )
        o_ref[:, cols] = jnp.where(keep, out, F32(0.0)).astype(BF16)


VMEM = pl.BlockSpec(memory_space=pltpu.VMEM)
PARAMS = pltpu.CompilerParams(vmem_limit_bytes=40 << 20)


def over_prompt(kernel, n_out, qs, kvs, own, *more):
    work = n_out * TOKENS * HEADS * sum(kv.shape[0] // 2 for kv in kvs)
    return pl.pallas_call(
        functools.partial(kernel, len(kvs)),
        out_shape=[jax.ShapeDtypeStruct((TOKENS, (HEADS + 1) * WIDTH), BF16)] * n_out,
        in_specs=[VMEM] * (len(qs) + len(kvs) + len(own) + len(more)),
        out_specs=[VMEM] * n_out,
        compiler_params=PARAMS,
        cost_estimate=pl.CostEstimate(
            flops=work * WIDTH * 8, bytes_accessed=2 << 20, transcendentals=work
        ),
        name="over_prompt",
    )(*qs, *kvs, *own, *more)


def merge(q, parts):
    return pl.pallas_call(
        functools.partial(merge_kernel, len(parts)),
        out_shape=jax.ShapeDtypeStruct((TOKENS, HEADS * WIDTH), BF16),
        in_specs=[VMEM] * (1 + len(parts)),
        out_specs=VMEM,
        compiler_params=PARAMS,
        name="merge",
    )(q, *parts)


def shards(
    answer_probe_vectors,
    answer_lookup_vectors,
    answer_content_vectors,
    common_context_lookups,
    common_context_contents,
    place_answer_number,
    answer_token_count,
    passing_answers,
):
    mine = jnp.arange(place_answer_number.shape[0]) == lax.axis_index("blk")
    kept = mine & (place_answer_number < passing_answers)
    count = jnp.where(kept, answer_token_count, 0).astype(BF16)
    count = jnp.pad(count, (0, HEADS * WIDTH - count.shape[0]))
    q = jnp.concatenate([answer_probe_vectors[0], jnp.broadcast_to(count, (16, count.shape[0]))], 0)
    kv = jnp.concatenate([common_context_lookups, common_context_contents], 0)
    qs, kvs = {0: q}, {(0, 0): kv}
    for bits in (2, 1, 3):
        qs[bits] = swapped(q, bits, 0, 0)
        kvs[bits, 0] = swapped(kv, 0, bits, 0)
    for bits in (0, 1, 3, 2):
        kvs[bits, 1] = swapped(kvs[bits, 0], 0, 0, 1)
    every = list(kvs.values())
    own = (answer_lookup_vectors[0], answer_content_vectors[0])
    part_far, part_own = over_prompt(far_kernel, 2, [q, qs[2]], every, own)
    all_q = [q, qs[2], qs[1], qs[3]]
    part_a, part_b, part_own = over_prompt(near_kernel, 3, all_q, every, own, part_own)
    (part_own,) = over_prompt(own_kernel, 1, all_q, every, own, part_own)
    parts = [swapped(part_far, 2, 0, 0), swapped(part_a, 1, 0, 0), swapped(part_b, 3, 0, 0)]
    return merge(q, [part_own, *parts])[None]


def solution(mesh):
    placed = (
        P(("grp", "blk"), None, "head"),
        P(("grp", "blk"), None, "head"),
        P(("grp", "blk"), None, "head"),
        P(("grp", "blk"), "head"),
        P(("grp", "blk"), "head"),
        P("grp"),
        P(("grp", "blk")),
        P("grp"),
    )
    return jax.shard_map(
        shards,
        mesh=mesh,
        in_specs=placed,
        out_specs=P(("grp", "blk"), None, "head"),
        check_vma=False,
    )
```

profile of v0, /device:TPU:224, one launch (start us, length us, event | category | flops | bytes accessed | tf_op | source)
XLA Modules:
  0.0 50.4 jit_solution(14620653450889950880)
XLA Ops:
  0.0 0.0 copy-start.3
  0.0 0.0 copy-start.2
  0.0 1.0 %constant_dynamic-update-slice_fusion.1 = bf16[1024,128]{1,0:T(8,128)(2,1)S(1)} fusion(bf16[512,128]{1,0:T(8,128)(2,1)} %param.11), kind=kLoop, calls=%fused_computation.2 | loop fusion | bytes 262144
  1.0 0.0 copy-done.3
  1.0 2.8 %collective-permute-start.5 = (bf16[1024,128]{1,0:T(8,128)(2,1)S(1)}, bf16[1024,128]{1,0:T(8,128)(2,1)S(1)}, u32[]{:S(2)}, u32[]{:S(2)}) collective-permute-start(bf16[1024,128]{1,0:T(8,128)(2,1)S(1)} %constant_dynamic-update-slice_fusion.refs_0_), channel_id=1, source_target_pairs={{0,48},{8,56},{16,32},{24,40},{32,16},{40,24},{48,0},{56,8},{64,11... | collective-permute-start | bytes 786440 | tf_op jit(solution)/shard_map/ppermute | solution.py:32
  3.9 0.2 collective-permute-start.4
  4.1 1.7 %collective-permute-start.3 = (bf16[1024,128]{1,0:T(8,128)(2,1)S(1)}, bf16[1024,128]{1,0:T(8,128)(2,1)S(1)}, u32[]{:S(2)}, u32[]{:S(2)}) collective-permute-start(bf16[1024,128]{1,0:T(8,128)(2,1)S(1)} %constant_dynamic-update-slice_fusion.refs_0_), channel_id=1, source_target_pairs={{0,32},{8,40},{16,48},{24,56},{32,0},{40,8},{48,16},{56,24},{64,96... | collective-permute-start | bytes 786440 | tf_op jit(solution)/shard_map/ppermute | solution.py:32
  7.1 0.0 copy-start.4
  7.1 0.6 %copy-done.4 = s32[32]{0:T(128)S(1)} copy-done((s32[32]{0:T(128)S(1)}, s32[32]{0:T(128)}, u32[]{:S(2)}) %copy-start.4) | copy-done | bytes 152
  7.8 0.0 copy-done.2
  7.8 0.0 copy-start
  7.8 0.0 copy-start.1
  7.8 3.3 %collective-permute-start = (bf16[144,1024]{1,0:T(8,128)(2,1)S(1)}, bf16[144,1024]{1,0:T(8,128)(2,1)S(1)}, u32[]{:S(2)}, u32[]{:S(2)}) collective-permute-start(bf16[144,1024]{1,0:T(8,128)(2,1)S(1)} %pad_maximum_fusion.q_ref), channel_id=1, source_target_pairs={{0,128},{8,136},{16,144},{24,152},{32,160},{40,168},{48,176},{56,1... | collective-permute-start | bytes 884744 | tf_op jit(solution)/shard_map/ppermute | solution.py:32
  11.1 0.0 collective-permute-start.6
  11.1 0.0 collective-permute-done.5.refs_3_
  11.1 0.5 %collective-permute-start.8 = (bf16[1024,128]{1,0:T(8,128)(2,1)S(1)}, bf16[1024,128]{1,0:T(8,128)(2,1)S(1)}, u32[]{:S(2)}, u32[]{:S(2)}) collective-permute-start(bf16[1024,128]{1,0:T(8,128)(2,1)S(1)} %collective-permute-done.5.refs_3_), channel_id=1, source_target_pairs={{0,8},{8,0},{16,24},{24,16},{32,40},{40,32},{48,56},{56,48},{64,72... | collective-permute-start | bytes 786440 | tf_op jit(solution)/shard_map/ppermute | solution.py:32
  11.6 1.4 %collective-permute-done.4.refs_2_ = bf16[1024,128]{1,0:T(8,128)(2,1)S(1)} collective-permute-done((bf16[1024,128]{1,0:T(8,128)(2,1)S(1)}, bf16[1024,128]{1,0:T(8,128)(2,1)S(1)}, u32[]{:S(2)}, u32[]{:S(2)}) %collective-permute-start.4) | collective-permute-done | bytes 262176 | tf_op jit(solution)/shard_map/ppermute | solution.py:32
  13.1 0.0 collective-permute-start.7
  13.1 4.1 %collective-permute-done.3.refs_1_ = bf16[1024,128]{1,0:T(8,128)(2,1)S(1)} collective-permute-done((bf16[1024,128]{1,0:T(8,128)(2,1)S(1)}, bf16[1024,128]{1,0:T(8,128)(2,1)S(1)}, u32[]{:S(2)}, u32[]{:S(2)}) %collective-permute-start.3) | collective-permute-done | bytes 262176 | tf_op jit(solution)/shard_map/ppermute | solution.py:32
  17.2 0.0 collective-permute-start.9
  17.2 0.0 collective-permute-done.6.refs_4_
  17.2 3.0 %collective-permute-start.2 = (bf16[144,1024]{1,0:T(8,128)(2,1)S(1)}, bf16[144,1024]{1,0:T(8,128)(2,1)S(1)}, u32[]{:S(2)}, u32[]{:S(2)}) collective-permute-start(bf16[144,1024]{1,0:T(8,128)(2,1)S(1)} %pad_maximum_fusion.q_ref), channel_id=1, source_target_pairs={{0,192},{8,200},{16,208},{24,216},{32,224},{40,232},{48,240},{56,2... | collective-permute-start | bytes 884744 | tf_op jit(solution)/shard_map/ppermute | solution.py:32
  20.2 0.0 collective-permute-done.q_far_ref
  20.2 0.1 collective-permute-start.1
  20.3 0.0 collective-permute-done.8.refs_6_
  20.3 0.0 collective-permute-done.7.refs_5_
  20.3 0.0 collective-permute-done.9.refs_7_
  20.3 0.0 copy-done
  20.3 0.0 copy-done.1
  20.4 5.6 %over_prompt.3 = (bf16[128,1152]{1,0:T(8,128)(2,1)S(1)}, bf16[128,1152]{1,0:T(8,128)(2,1)S(1)}) custom-call(bf16[144,1024]{1,0:T(8,128)(2,1)S(1)} %pad_maximum_fusion.q_ref, bf16[144,1024]{1,0:T(8,128)(2,1)S(1)} %collective-permute-done.q_far_ref, bf16[1024,128]{1,0:T(8,128)(2,1)S(1)} %constant_dynamic-update-slice_fusion.refs_0_, ...), custom_call_target="tpu_custom_call" | custom-call | flops 8589934592 | bytes 2097152 | tf_op jit(solution)/shard_map/over_prompt/pallas_call | solution.py:200
  26.0 1.6 %collective-permute-start.10 = (bf16[128,1152]{1,0:T(8,128)(2,1)S(1)}, bf16[128,1152]{1,0:T(8,128)(2,1)S(1)}, u32[]{:S(2)}, u32[]{:S(2)}) collective-permute-start(bf16[128,1152]{1,0:T(8,128)(2,1)S(1)} %get-tuple-element.12), channel_id=1, source_target_pairs={{0,128},{8,136},{16,144},{24,152},{32,160},{40,168},{48,176},{56,1... | collective-permute-start | bytes 884744 | tf_op jit(solution)/shard_map/ppermute | solution.py:32
  27.6 0.2 collective-permute-done.2.q_b_ref
  27.9 2.2 %collective-permute-done.1.q_a_ref = bf16[144,1024]{1,0:T(8,128)(2,1)S(1)} collective-permute-done((bf16[144,1024]{1,0:T(8,128)(2,1)S(1)}, bf16[144,1024]{1,0:T(8,128)(2,1)S(1)}, u32[]{:S(2)}, u32[]{:S(2)}) %collective-permute-start.1) | collective-permute-done | bytes 294944 | tf_op jit(solution)/shard_map/ppermute | solution.py:32
  30.0 10.7 %over_prompt.4 = (bf16[128,1152]{1,0:T(8,128)(2,1)S(1)}, bf16[128,1152]{1,0:T(8,128)(2,1)S(1)}, bf16[128,1152]{1,0:T(8,128)(2,1)S(1)}) custom-call(bf16[144,1024]{1,0:T(8,128)(2,1)S(1)} %pad_maximum_fusion.q_ref, bf16[144,1024]{1,0:T(8,128)(2,1)S(1)} %collective-permute-done.q_far_ref, bf16[144,1024]{1,0:T(8,128)(2,1)S(1)} %collective-permute-done.1.q_a_ref, ...), custom_call_target="tpu_custom_call" | custom-call | flops 12884901888 | bytes 2097152 | tf_op jit(solution)/shard_map/over_prompt/pallas_call | solution.py:200
  40.7 0.1 collective-permute-start.11
  40.8 1.2 %collective-permute-start.12 = (bf16[128,1152]{1,0:T(8,128)(2,1)S(1)}, bf16[128,1152]{1,0:T(8,128)(2,1)S(1)}, u32[]{:S(2)}, u32[]{:S(2)}) collective-permute-start(bf16[128,1152]{1,0:T(8,128)(2,1)S(1)} %get-tuple-element.14), channel_id=1, source_target_pairs={{0,192},{8,200},{16,208},{24,216},{32,224},{40,232},{48,240},{56,2... | collective-permute-start | bytes 884744 | tf_op jit(solution)/shard_map/ppermute | solution.py:32
  42.0 0.4 over_prompt.5.refs_0_
  42.5 0.0 collective-permute-done.10.refs_1_
  42.5 5.1 %collective-permute-done.11.refs_2_ = bf16[128,1152]{1,0:T(8,128)(2,1)S(1)} collective-permute-done((bf16[128,1152]{1,0:T(8,128)(2,1)S(1)}, bf16[128,1152]{1,0:T(8,128)(2,1)S(1)}, u32[]{:S(2)}, u32[]{:S(2)}) %collective-permute-start.11) | collective-permute-done | bytes 294944 | tf_op jit(solution)/shard_map/ppermute | solution.py:32
  47.5 1.3 %collective-permute-done.12.refs_3_ = bf16[128,1152]{1,0:T(8,128)(2,1)S(1)} collective-permute-done((bf16[128,1152]{1,0:T(8,128)(2,1)S(1)}, bf16[128,1152]{1,0:T(8,128)(2,1)S(1)}, u32[]{:S(2)}, u32[]{:S(2)}) %collective-permute-start.12) | collective-permute-done | bytes 294944 | tf_op jit(solution)/shard_map/ppermute | solution.py:32
  48.9 1.5 %merge.1 = bf16[128,1024]{1,0:T(8,128)(2,1)} custom-call(bf16[144,1024]{1,0:T(8,128)(2,1)S(1)} %pad_maximum_fusion.q_ref, bf16[128,1152]{1,0:T(8,128)(2,1)S(1)} %over_prompt.5.refs_0_, bf16[128,1152]{1,0:T(8,128)(2,1)S(1)} %collective-permute-done.10.refs_1_, bf16[128,1152]{1,0:T(8,128)(2,1)S(1)} %collective-permute-done.11.refs_2_, ...), custom_call_target="tpu_custom_call" | custom-call | tf_op jit(solution)/shard_map/merge/pallas_call | solution.py:214
  (5 shorter events, 0.1 us)
Async XLA Ops:
  0.0 1.0 %copy-start.3 = (bf16[512,128]{1,0:T(8,128)(2,1)S(1)}, bf16[512,128]{1,0:T(8,128)(2,1)}, u32[]{:S(2)}) copy-start(bf16[512,128]{1,0:T(8,128)(2,1)} %param.12) | copy-start | bytes 393220
  0.0 7.8 %copy-start.2 = (bf16[1,128,1024]{2,1,0:T(8,128)(2,1)S(1)}, bf16[1,128,1024]{2,1,0:T(8,128)(2,1)}, u32[]{:S(2)}) copy-start(bf16[1,128,1024]{2,1,0:T(8,128)(2,1)} %param.8) | copy-start | bytes 786436
  1.0 10.1 %collective-permute-start.5 = (bf16[1024,128]{1,0:T(8,128)(2,1)S(1)}, bf16[1024,128]{1,0:T(8,128)(2,1)S(1)}, u32[]{:S(2)}, u32[]{:S(2)}) collective-permute-start(bf16[1024,128]{1,0:T(8,128)(2,1)S(1)} %constant_dynamic-update-slice_fusion.refs_0_), channel_id=1, source_target_pairs={{0,48},{8,56},{16,32},{24,40},{32,16},{40,24},{48,0},{56,8},{64,11... | collective-permute-start | bytes 786440 | tf_op jit(solution)/shard_map/ppermute | solution.py:32
  3.9 9.2 %collective-permute-start.4 = (bf16[1024,128]{1,0:T(8,128)(2,1)S(1)}, bf16[1024,128]{1,0:T(8,128)(2,1)S(1)}, u32[]{:S(2)}, u32[]{:S(2)}) collective-permute-start(bf16[1024,128]{1,0:T(8,128)(2,1)S(1)} %constant_dynamic-update-slice_fusion.refs_0_), channel_id=1, source_target_pairs={{0,16},{8,24},{16,0},{24,8},{32,48},{40,56},{48,32},{56,40},{64,80... | collective-permute-start | bytes 786440 | tf_op jit(solution)/shard_map/ppermute | solution.py:32
  4.1 13.1 %collective-permute-start.3 = (bf16[1024,128]{1,0:T(8,128)(2,1)S(1)}, bf16[1024,128]{1,0:T(8,128)(2,1)S(1)}, u32[]{:S(2)}, u32[]{:S(2)}) collective-permute-start(bf16[1024,128]{1,0:T(8,128)(2,1)S(1)} %constant_dynamic-update-slice_fusion.refs_0_), channel_id=1, source_target_pairs={{0,32},{8,40},{16,48},{24,56},{32,0},{40,8},{48,16},{56,24},{64,96... | collective-permute-start | bytes 786440 | tf_op jit(solution)/shard_map/ppermute | solution.py:32
  7.1 0.7 %copy-start.4 = (s32[32]{0:T(128)S(1)}, s32[32]{0:T(128)}, u32[]{:S(2)}) copy-start(s32[32]{0:T(128)} %param.13) | copy-start | bytes 388
  7.8 12.5 %copy-start = (bf16[1,128,128]{2,1,0:T(8,128)(2,1)S(1)}, bf16[1,128,128]{2,1,0:T(8,128)(2,1)}, u32[]{:S(2)}) copy-start(bf16[1,128,128]{2,1,0:T(8,128)(2,1)} %param.9) | copy-start | bytes 98308
  7.8 12.5 %copy-start.1 = (bf16[1,128,128]{2,1,0:T(8,128)(2,1)S(1)}, bf16[1,128,128]{2,1,0:T(8,128)(2,1)}, u32[]{:S(2)}) copy-start(bf16[1,128,128]{2,1,0:T(8,128)(2,1)} %param.10) | copy-start | bytes 98308
  7.8 12.3 %collective-permute-start = (bf16[144,1024]{1,0:T(8,128)(2,1)S(1)}, bf16[144,1024]{1,0:T(8,128)(2,1)S(1)}, u32[]{:S(2)}, u32[]{:S(2)}) collective-permute-start(bf16[144,1024]{1,0:T(8,128)(2,1)S(1)} %pad_maximum_fusion.q_ref), channel_id=1, source_target_pairs={{0,128},{8,136},{16,144},{24,152},{32,160},{40,168},{48,176},{56,1... | collective-permute-start | bytes 884744 | tf_op jit(solution)/shard_map/ppermute | solution.py:32
  11.1 6.0 %collective-permute-start.6 = (bf16[1024,128]{1,0:T(8,128)(2,1)S(1)}, bf16[1024,128]{1,0:T(8,128)(2,1)S(1)}, u32[]{:S(2)}, u32[]{:S(2)}) collective-permute-start(bf16[1024,128]{1,0:T(8,128)(2,1)S(1)} %constant_dynamic-update-slice_fusion.refs_0_), channel_id=1, source_target_pairs={{0,8},{8,0},{16,24},{24,16},{32,40},{40,32},{48,56},{56,48},{64,72... | collective-permute-start | bytes 786440 | tf_op jit(solution)/shard_map/ppermute | solution.py:32
  11.1 9.2 %collective-permute-start.8 = (bf16[1024,128]{1,0:T(8,128)(2,1)S(1)}, bf16[1024,128]{1,0:T(8,128)(2,1)S(1)}, u32[]{:S(2)}, u32[]{:S(2)}) collective-permute-start(bf16[1024,128]{1,0:T(8,128)(2,1)S(1)} %collective-permute-done.5.refs_3_), channel_id=1, source_target_pairs={{0,8},{8,0},{16,24},{24,16},{32,40},{40,32},{48,56},{56,48},{64,72... | collective-permute-start | bytes 786440 | tf_op jit(solution)/shard_map/ppermute | solution.py:32
  13.1 7.2 %collective-permute-start.7 = (bf16[1024,128]{1,0:T(8,128)(2,1)S(1)}, bf16[1024,128]{1,0:T(8,128)(2,1)S(1)}, u32[]{:S(2)}, u32[]{:S(2)}) collective-permute-start(bf16[1024,128]{1,0:T(8,128)(2,1)S(1)} %collective-permute-done.4.refs_2_), channel_id=1, source_target_pairs={{0,8},{8,0},{16,24},{24,16},{32,40},{40,32},{48,56},{56,48},{64,72... | collective-permute-start | bytes 786440 | tf_op jit(solution)/shard_map/ppermute | solution.py:32
  17.2 3.2 %collective-permute-start.9 = (bf16[1024,128]{1,0:T(8,128)(2,1)S(1)}, bf16[1024,128]{1,0:T(8,128)(2,1)S(1)}, u32[]{:S(2)}, u32[]{:S(2)}) collective-permute-start(bf16[1024,128]{1,0:T(8,128)(2,1)S(1)} %collective-permute-done.3.refs_1_), channel_id=1, source_target_pairs={{0,8},{8,0},{16,24},{24,16},{32,40},{40,32},{48,56},{56,48},{64,72... | collective-permute-start | bytes 786440 | tf_op jit(solution)/shard_map/ppermute | solution.py:32
  17.2 10.7 %collective-permute-start.2 = (bf16[144,1024]{1,0:T(8,128)(2,1)S(1)}, bf16[144,1024]{1,0:T(8,128)(2,1)S(1)}, u32[]{:S(2)}, u32[]{:S(2)}) collective-permute-start(bf16[144,1024]{1,0:T(8,128)(2,1)S(1)} %pad_maximum_fusion.q_ref), channel_id=1, source_target_pairs={{0,192},{8,200},{16,208},{24,216},{32,224},{40,232},{48,240},{56,2... | collective-permute-start | bytes 884744 | tf_op jit(solution)/shard_map/ppermute | solution.py:32
  20.2 9.8 %collective-permute-start.1 = (bf16[144,1024]{1,0:T(8,128)(2,1)S(1)}, bf16[144,1024]{1,0:T(8,128)(2,1)S(1)}, u32[]{:S(2)}, u32[]{:S(2)}) collective-permute-start(bf16[144,1024]{1,0:T(8,128)(2,1)S(1)} %pad_maximum_fusion.q_ref), channel_id=1, source_target_pairs={{0,64},{8,72},{16,80},{24,88},{32,96},{40,104},{48,112},{56,120},{... | collective-permute-start | bytes 884744 | tf_op jit(solution)/shard_map/ppermute | solution.py:32
  26.0 16.5 %collective-permute-start.10 = (bf16[128,1152]{1,0:T(8,128)(2,1)S(1)}, bf16[128,1152]{1,0:T(8,128)(2,1)S(1)}, u32[]{:S(2)}, u32[]{:S(2)}) collective-permute-start(bf16[128,1152]{1,0:T(8,128)(2,1)S(1)} %get-tuple-element.12), channel_id=1, source_target_pairs={{0,128},{8,136},{16,144},{24,152},{32,160},{40,168},{48,176},{56,1... | collective-permute-start | bytes 884744 | tf_op jit(solution)/shard_map/ppermute | solution.py:32
  40.7 6.8 %collective-permute-start.11 = (bf16[128,1152]{1,0:T(8,128)(2,1)S(1)}, bf16[128,1152]{1,0:T(8,128)(2,1)S(1)}, u32[]{:S(2)}, u32[]{:S(2)}) collective-permute-start(bf16[128,1152]{1,0:T(8,128)(2,1)S(1)} %get-tuple-element.13), channel_id=1, source_target_pairs={{0,64},{8,72},{16,80},{24,88},{32,96},{40,104},{48,112},{56,120},{... | collective-permute-start | bytes 884744 | tf_op jit(solution)/shard_map/ppermute | solution.py:32
  40.8 8.0 %collective-permute-start.12 = (bf16[128,1152]{1,0:T(8,128)(2,1)S(1)}, bf16[128,1152]{1,0:T(8,128)(2,1)S(1)}, u32[]{:S(2)}, u32[]{:S(2)}) collective-permute-start(bf16[128,1152]{1,0:T(8,128)(2,1)S(1)} %get-tuple-element.14), channel_id=1, source_target_pairs={{0,192},{8,200},{16,208},{24,216},{32,224},{40,232},{48,240},{56,2... | collective-permute-start | bytes 884744 | tf_op jit(solution)/shard_map/ppermute | solution.py:32
where the time goes:
time: 50.5 us; the launch traced here: 50.4 us
  Pallas kernels  18.3 us (36%)
  starting transfers between devices  14.7 us (29%)
  waiting for transfers between devices  14.3 us (28%)
  local copies, waits for them, and re-layouts  1.67 us (3%)
  between operations  1.43 us (3%)
    pallas_call x3, Pallas kernels, over_prompt(): pl.pallas_call(functools.partial(kernel, len(kvs)), out_shape=[jax.ShapeD...  16.7 us
    ppermute x13, starting transfers between devices, swapped(): return lax.ppermute(block, 'blk', route)  14.7 us
    ppermute x13, waiting for transfers between devices, swapped(): return lax.ppermute(block, 'blk', route)  14.3 us
    unnamed x11, local copies, waits for them, and re-layouts  1.63 us
    pallas_call x1, Pallas kernels, merge(): pl.pallas_call(functools.partial(merge_kernel, len(parts)), out_shape=jax...  1.53 us
  transfers between devices with their start and end apart: 13, of which 6 were waited for; matrix products, arithmetic and copies ran while one was open for 0% of the time, Pallas kernels for 33%

commit v1 on v0

--- a/solution.py
+++ b/solution.py
@@ -167,28 +167,37 @@
 
 
 def merge_kernel(n, q_ref, *refs):
-    part_refs, o_ref = refs[:n], refs[n]
+    part_refs, (o_ref, held, sems) = refs[:n], refs[n:]
     count = kept_tokens(q_ref)
-    keep = lax.broadcasted_iota(jnp.int32, (TOKENS, WIDTH), 0) < count
-    lses = []
-    for ref in part_refs:
-        stats = ref[:, HEADS * WIDTH :].astype(F32)
-        lses.append(
-            stats
-            + pltpu.roll(stats, WIDTH - HEADS, 1)
-            + pltpu.roll(stats, WIDTH - 2 * HEADS, 1)
-        )
-    peak = functools.reduce(jnp.maximum, lses)
-    weights = [jnp.exp2(v - peak) for v in lses]
-    inverse = 1.0 / sum(weights)
-    weights = [w * inverse for w in weights]
-    for h in range(HEADS):
-        cols = slice(h * WIDTH, (h + 1) * WIDTH)
-        out = sum(
-            ref[:, cols].astype(F32) * w[:, h : h + 1]
-            for ref, w in zip(part_refs, weights, strict=True)
-        )
-        o_ref[:, cols] = jnp.where(keep, out, F32(0.0)).astype(BF16)
+    half = TOKENS // 2
+    copies = []
+    for i in range(2):
+        at = slice(i * half, (i + 1) * half)
+        keep = lax.broadcasted_iota(jnp.int32, (half, WIDTH), 0) + i * half < count
+        lses = []
+        for ref in part_refs:
+            stats = ref[at, HEADS * WIDTH :].astype(F32)
+            lses.append(
+                stats
+                + pltpu.roll(stats, WIDTH - HEADS, 1)
+                + pltpu.roll(stats, WIDTH - 2 * HEADS, 1)
+            )
+        peak = functools.reduce(jnp.maximum, lses)
+        weights = [jnp.exp2(v - peak) for v in lses]
+        inverse = 1.0 / sum(weights)
+        weights = [w * inverse for w in weights]
+        for h in range(HEADS):
+            cols = slice(h * WIDTH, (h + 1) * WIDTH)
+            out = sum(
+                ref[at, cols].astype(F32) * w[:, h : h + 1]
+                for ref, w in zip(part_refs, weights, strict=True)
+            )
+            held[at, cols] = jnp.where(keep, out, F32(0.0)).astype(BF16)
+        copy = pltpu.make_async_copy(held.at[at, :], o_ref.at[at, :], sems.at[i])
+        copy.start()
+        copies.append(copy)
+    for copy in copies:
+        copy.wait()
 
 
 VMEM = pl.BlockSpec(memory_space=pltpu.VMEM)
@@ -215,7 +224,11 @@
         functools.partial(merge_kernel, len(parts)),
         out_shape=jax.ShapeDtypeStruct((TOKENS, HEADS * WIDTH), BF16),
         in_specs=[VMEM] * (1 + len(parts)),
-        out_specs=VMEM,
+        out_specs=pl.BlockSpec(memory_space=pl.ANY),
+        scratch_shapes=[
+            pltpu.VMEM((TOKENS, HEADS * WIDTH), BF16),
+            pltpu.SemaphoreType.DMA((2,)),
+        ],
         compiler_params=PARAMS,
         name="merge",
     )(q, *parts)

time: 50.5 us -> 50.6 us (level)
  the two profiles are of different devices: /device:TPU:224 before, /device:TPU:134 now
where the time goes in v1:
time: 50.6 us; the launch traced here: 51.1 us
  Pallas kernels  16.7 us (33%)
  waiting for transfers between devices  16 us (32%)
  starting transfers between devices  15.1 us (30%)
  local copies, waits for them, and re-layouts  1.67 us (3%)
  between operations  1.63 us (3%)
    ppermute x13, waiting for transfers between devices, swapped(): return lax.ppermute(block, 'blk', route)  16 us
    ppermute x13, starting transfers between devices, swapped(): return lax.ppermute(block, 'blk', route)  15.1 us
    pallas_call x3, Pallas kernels, over_prompt(): pl.pallas_call(functools.partial(kernel, len(kvs)), out_shape=[jax.ShapeD...  14.9 us
    pallas_call x1, Pallas kernels, merge(): pl.pallas_call(functools.partial(merge_kernel, len(parts)), out_shape=jax...  1.79 us
    unnamed x11, local copies, waits for them, and re-layouts  1.63 us
  transfers between devices with their start and end apart: 13, of which 5 were waited for; matrix products, arithmetic and copies ran while one was open for 0% of the time, Pallas kernels for 29%

profile of v1, /device:TPU:134, one launch (start us, length us, event | category | flops | bytes accessed | tf_op | source)
XLA Modules:
  0.0 51.1 jit_solution(4898136357642685015)
XLA Ops:
  0.0 0.0 copy-start.3
  0.0 0.0 copy-start.2
  0.0 1.0 %constant_dynamic-update-slice_fusion.1 = bf16[1024,128]{1,0:T(8,128)(2,1)S(1)} fusion(bf16[512,128]{1,0:T(8,128)(2,1)} %param.11), kind=kLoop, calls=%fused_computation.2 | loop fusion | bytes 262144
  1.0 0.0 copy-done.3
  1.0 0.6 %collective-permute-start.5 = (bf16[1024,128]{1,0:T(8,128)(2,1)S(1)}, bf16[1024,128]{1,0:T(8,128)(2,1)S(1)}, u32[]{:S(2)}, u32[]{:S(2)}) collective-permute-start(bf16[1024,128]{1,0:T(8,128)(2,1)S(1)} %constant_dynamic-update-slice_fusion.refs_0_), channel_id=1, source_target_pairs={{0,48},{8,56},{16,32},{24,40},{32,16},{40,24},{48,0},{56,8},{64,11... | collective-permute-start | bytes 786440 | tf_op jit(solution)/shard_map/ppermute | solution.py:32
  1.6 0.9 %collective-permute-start.4 = (bf16[1024,128]{1,0:T(8,128)(2,1)S(1)}, bf16[1024,128]{1,0:T(8,128)(2,1)S(1)}, u32[]{:S(2)}, u32[]{:S(2)}) collective-permute-start(bf16[1024,128]{1,0:T(8,128)(2,1)S(1)} %constant_dynamic-update-slice_fusion.refs_0_), channel_id=1, source_target_pairs={{0,16},{8,24},{16,0},{24,8},{32,48},{40,56},{48,32},{56,40},{64,80... | collective-permute-start | bytes 786440 | tf_op jit(solution)/shard_map/ppermute | solution.py:32
  2.5 3.3 %collective-permute-start.3 = (bf16[1024,128]{1,0:T(8,128)(2,1)S(1)}, bf16[1024,128]{1,0:T(8,128)(2,1)S(1)}, u32[]{:S(2)}, u32[]{:S(2)}) collective-permute-start(bf16[1024,128]{1,0:T(8,128)(2,1)S(1)} %constant_dynamic-update-slice_fusion.refs_0_), channel_id=1, source_target_pairs={{0,32},{8,40},{16,48},{24,56},{32,0},{40,8},{48,16},{56,24},{64,96... | collective-permute-start | bytes 786440 | tf_op jit(solution)/shard_map/ppermute | solution.py:32
  7.1 0.0 copy-start.4
  7.1 0.6 %copy-done.4 = s32[32]{0:T(128)S(1)} copy-done((s32[32]{0:T(128)S(1)}, s32[32]{0:T(128)}, u32[]{:S(2)}) %copy-start.4) | copy-done | bytes 152
  7.8 0.0 copy-done.2
  7.8 0.0 copy-start
  7.8 0.0 copy-start.1
  7.8 3.3 %collective-permute-start = (bf16[144,1024]{1,0:T(8,128)(2,1)S(1)}, bf16[144,1024]{1,0:T(8,128)(2,1)S(1)}, u32[]{:S(2)}, u32[]{:S(2)}) collective-permute-start(bf16[144,1024]{1,0:T(8,128)(2,1)S(1)} %pad_maximum_fusion.q_ref), channel_id=1, source_target_pairs={{0,128},{8,136},{16,144},{24,152},{32,160},{40,168},{48,176},{56,1... | collective-permute-start | bytes 884744 | tf_op jit(solution)/shard_map/ppermute | solution.py:32
  11.1 0.0 collective-permute-start.6
  11.1 0.0 collective-permute-done.5.refs_3_
  11.1 0.5 collective-permute-start.8
  11.6 0.0 collective-permute-done.4.refs_2_
  11.6 0.1 collective-permute-start.7
  11.7 5.4 %collective-permute-done.3.refs_1_ = bf16[1024,128]{1,0:T(8,128)(2,1)S(1)} collective-permute-done((bf16[1024,128]{1,0:T(8,128)(2,1)S(1)}, bf16[1024,128]{1,0:T(8,128)(2,1)S(1)}, u32[]{:S(2)}, u32[]{:S(2)}) %collective-permute-start.3) | collective-permute-done | bytes 262176 | tf_op jit(solution)/shard_map/ppermute | solution.py:32
  17.2 0.0 collective-permute-start.9
  17.2 0.0 collective-permute-done.6.refs_4_
  17.2 3.0 %collective-permute-start.2 = (bf16[144,1024]{1,0:T(8,128)(2,1)S(1)}, bf16[144,1024]{1,0:T(8,128)(2,1)S(1)}, u32[]{:S(2)}, u32[]{:S(2)}) collective-permute-start(bf16[144,1024]{1,0:T(8,128)(2,1)S(1)} %pad_maximum_fusion.q_ref), channel_id=1, source_target_pairs={{0,192},{8,200},{16,208},{24,216},{32,224},{40,232},{48,240},{56,2... | collective-permute-start | bytes 884744 | tf_op jit(solution)/shard_map/ppermute | solution.py:32
  20.2 0.0 collective-permute-done.q_far_ref
  20.2 0.1 collective-permute-start.1
  20.3 0.0 collective-permute-done.8.refs_6_
  20.3 0.0 collective-permute-done.7.refs_5_
  20.3 0.0 collective-permute-done.9.refs_7_
  20.3 0.0 copy-done
  20.3 0.0 copy-done.1
  20.4 4.5 %over_prompt.3 = (bf16[128,1152]{1,0:T(8,128)(2,1)S(1)}, bf16[128,1152]{1,0:T(8,128)(2,1)S(1)}) custom-call(bf16[144,1024]{1,0:T(8,128)(2,1)S(1)} %pad_maximum_fusion.q_ref, bf16[144,1024]{1,0:T(8,128)(2,1)S(1)} %collective-permute-done.q_far_ref, bf16[1024,128]{1,0:T(8,128)(2,1)S(1)} %constant_dynamic-update-slice_fusion.refs_0_, ...), custom_call_target="tpu_custom_call" | custom-call | flops 8589934592 | bytes 2097152 | tf_op jit(solution)/shard_map/over_prompt/pallas_call | solution.py:209
  24.9 2.2 %collective-permute-start.10 = (bf16[128,1152]{1,0:T(8,128)(2,1)S(1)}, bf16[128,1152]{1,0:T(8,128)(2,1)S(1)}, u32[]{:S(2)}, u32[]{:S(2)}) collective-permute-start(bf16[128,1152]{1,0:T(8,128)(2,1)S(1)} %get-tuple-element.12), channel_id=1, source_target_pairs={{0,128},{8,136},{16,144},{24,152},{32,160},{40,168},{48,176},{56,1... | collective-permute-start | bytes 884744 | tf_op jit(solution)/shard_map/ppermute | solution.py:32
  27.1 0.8 %collective-permute-done.2.q_b_ref = bf16[144,1024]{1,0:T(8,128)(2,1)S(1)} collective-permute-done((bf16[144,1024]{1,0:T(8,128)(2,1)S(1)}, bf16[144,1024]{1,0:T(8,128)(2,1)S(1)}, u32[]{:S(2)}, u32[]{:S(2)}) %collective-permute-start.2) | collective-permute-done | bytes 294944 | tf_op jit(solution)/shard_map/ppermute | solution.py:32
  27.9 1.6 %collective-permute-done.1.q_a_ref = bf16[144,1024]{1,0:T(8,128)(2,1)S(1)} collective-permute-done((bf16[144,1024]{1,0:T(8,128)(2,1)S(1)}, bf16[144,1024]{1,0:T(8,128)(2,1)S(1)}, u32[]{:S(2)}, u32[]{:S(2)}) %collective-permute-start.1) | collective-permute-done | bytes 294944 | tf_op jit(solution)/shard_map/ppermute | solution.py:32
  29.5 9.9 %over_prompt.4 = (bf16[128,1152]{1,0:T(8,128)(2,1)S(1)}, bf16[128,1152]{1,0:T(8,128)(2,1)S(1)}, bf16[128,1152]{1,0:T(8,128)(2,1)S(1)}) custom-call(bf16[144,1024]{1,0:T(8,128)(2,1)S(1)} %pad_maximum_fusion.q_ref, bf16[144,1024]{1,0:T(8,128)(2,1)S(1)} %collective-permute-done.q_far_ref, bf16[144,1024]{1,0:T(8,128)(2,1)S(1)} %collective-permute-done.1.q_a_ref, ...), custom_call_target="tpu_custom_call" | custom-call | flops 12884901888 | bytes 2097152 | tf_op jit(solution)/shard_map/over_prompt/pallas_call | solution.py:209
  39.4 0.1 collective-permute-start.11
  39.5 1.0 %collective-permute-start.12 = (bf16[128,1152]{1,0:T(8,128)(2,1)S(1)}, bf16[128,1152]{1,0:T(8,128)(2,1)S(1)}, u32[]{:S(2)}, u32[]{:S(2)}) collective-permute-start(bf16[128,1152]{1,0:T(8,128)(2,1)S(1)} %get-tuple-element.14), channel_id=1, source_target_pairs={{0,192},{8,200},{16,208},{24,216},{32,224},{40,232},{48,240},{56,2... | collective-permute-start | bytes 884744 | tf_op jit(solution)/shard_map/ppermute | solution.py:32
  40.6 0.4 over_prompt.5.refs_0_
  41.0 0.0 collective-permute-done.10.refs_1_
  41.0 6.8 %collective-permute-done.11.refs_2_ = bf16[128,1152]{1,0:T(8,128)(2,1)S(1)} collective-permute-done((bf16[128,1152]{1,0:T(8,128)(2,1)S(1)}, bf16[128,1152]{1,0:T(8,128)(2,1)S(1)}, u32[]{:S(2)}, u32[]{:S(2)}) %collective-permute-start.11) | collective-permute-done | bytes 294944 | tf_op jit(solution)/shard_map/ppermute | solution.py:32
  47.8 1.3 %collective-permute-done.12.refs_3_ = bf16[128,1152]{1,0:T(8,128)(2,1)S(1)} collective-permute-done((bf16[128,1152]{1,0:T(8,128)(2,1)S(1)}, bf16[128,1152]{1,0:T(8,128)(2,1)S(1)}, u32[]{:S(2)}, u32[]{:S(2)}) %collective-permute-start.12) | collective-permute-done | bytes 294944 | tf_op jit(solution)/shard_map/ppermute | solution.py:32
  49.2 1.8 %merge.1 = bf16[128,1024]{1,0:T(8,128)(2,1)} custom-call(bf16[144,1024]{1,0:T(8,128)(2,1)S(1)} %pad_maximum_fusion.q_ref, bf16[128,1152]{1,0:T(8,128)(2,1)S(1)} %over_prompt.5.refs_0_, bf16[128,1152]{1,0:T(8,128)(2,1)S(1)} %collective-permute-done.10.refs_1_, bf16[128,1152]{1,0:T(8,128)(2,1)S(1)} %collective-permute-done.11.refs_2_, ...), custom_call_target="tpu_custom_call" | custom-call | tf_op jit(solution)/shard_map/merge/pallas_call | solution.py:223
  (5 shorter events, 0.1 us)
Async XLA Ops:
  0.0 1.0 %copy-start.3 = (bf16[512,128]{1,0:T(8,128)(2,1)S(1)}, bf16[512,128]{1,0:T(8,128)(2,1)}, u32[]{:S(2)}) copy-start(bf16[512,128]{1,0:T(8,128)(2,1)} %param.12) | copy-start | bytes 393220
  0.0 7.8 %copy-start.2 = (bf16[1,128,1024]{2,1,0:T(8,128)(2,1)S(1)}, bf16[1,128,1024]{2,1,0:T(8,128)(2,1)}, u32[]{:S(2)}) copy-start(bf16[1,128,1024]{2,1,0:T(8,128)(2,1)} %param.8) | copy-start | bytes 786436
  1.0 10.1 %collective-permute-start.5 = (bf16[1024,128]{1,0:T(8,128)(2,1)S(1)}, bf16[1024,128]{1,0:T(8,128)(2,1)S(1)}, u32[]{:S(2)}, u32[]{:S(2)}) collective-permute-start(bf16[1024,128]{1,0:T(8,128)(2,1)S(1)} %constant_dynamic-update-slice_fusion.refs_0_), channel_id=1, source_target_pairs={{0,48},{8,56},{16,32},{24,40},{32,16},{40,24},{48,0},{56,8},{64,11... | collective-permute-start | bytes 786440 | tf_op jit(solution)/shard_map/ppermute | solution.py:32
  1.6 10.1 %collective-permute-start.4 = (bf16[1024,128]{1,0:T(8,128)(2,1)S(1)}, bf16[1024,128]{1,0:T(8,128)(2,1)S(1)}, u32[]{:S(2)}, u32[]{:S(2)}) collective-permute-start(bf16[1024,128]{1,0:T(8,128)(2,1)S(1)} %constant_dynamic-update-slice_fusion.refs_0_), channel_id=1, source_target_pairs={{0,16},{8,24},{16,0},{24,8},{32,48},{40,56},{48,32},{56,40},{64,80... | collective-permute-start | bytes 786440 | tf_op jit(solution)/shard_map/ppermute | solution.py:32
  2.5 14.7 %collective-permute-start.3 = (bf16[1024,128]{1,0:T(8,128)(2,1)S(1)}, bf16[1024,128]{1,0:T(8,128)(2,1)S(1)}, u32[]{:S(2)}, u32[]{:S(2)}) collective-permute-start(bf16[1024,128]{1,0:T(8,128)(2,1)S(1)} %constant_dynamic-update-slice_fusion.refs_0_), channel_id=1, source_target_pairs={{0,32},{8,40},{16,48},{24,56},{32,0},{40,8},{48,16},{56,24},{64,96... | collective-permute-start | bytes 786440 | tf_op jit(solution)/shard_map/ppermute | solution.py:32
  7.1 0.7 %copy-start.4 = (s32[32]{0:T(128)S(1)}, s32[32]{0:T(128)}, u32[]{:S(2)}) copy-start(s32[32]{0:T(128)} %param.13) | copy-start | bytes 388
  7.8 12.5 %copy-start = (bf16[1,128,128]{2,1,0:T(8,128)(2,1)S(1)}, bf16[1,128,128]{2,1,0:T(8,128)(2,1)}, u32[]{:S(2)}) copy-start(bf16[1,128,128]{2,1,0:T(8,128)(2,1)} %param.9) | copy-start | bytes 98308
  7.8 12.5 %copy-start.1 = (bf16[1,128,128]{2,1,0:T(8,128)(2,1)S(1)}, bf16[1,128,128]{2,1,0:T(8,128)(2,1)}, u32[]{:S(2)}) copy-start(bf16[1,128,128]{2,1,0:T(8,128)(2,1)} %param.10) | copy-start | bytes 98308
  7.8 12.3 %collective-permute-start = (bf16[144,1024]{1,0:T(8,128)(2,1)S(1)}, bf16[144,1024]{1,0:T(8,128)(2,1)S(1)}, u32[]{:S(2)}, u32[]{:S(2)}) collective-permute-start(bf16[144,1024]{1,0:T(8,128)(2,1)S(1)} %pad_maximum_fusion.q_ref), channel_id=1, source_target_pairs={{0,128},{8,136},{16,144},{24,152},{32,160},{40,168},{48,176},{56,1... | collective-permute-start | bytes 884744 | tf_op jit(solution)/shard_map/ppermute | solution.py:32
  11.1 6.0 %collective-permute-start.6 = (bf16[1024,128]{1,0:T(8,128)(2,1)S(1)}, bf16[1024,128]{1,0:T(8,128)(2,1)S(1)}, u32[]{:S(2)}, u32[]{:S(2)}) collective-permute-start(bf16[1024,128]{1,0:T(8,128)(2,1)S(1)} %constant_dynamic-update-slice_fusion.refs_0_), channel_id=1, source_target_pairs={{0,8},{8,0},{16,24},{24,16},{32,40},{40,32},{48,56},{56,48},{64,72... | collective-permute-start | bytes 786440 | tf_op jit(solution)/shard_map/ppermute | solution.py:32
  11.1 9.2 %collective-permute-start.8 = (bf16[1024,128]{1,0:T(8,128)(2,1)S(1)}, bf16[1024,128]{1,0:T(8,128)(2,1)S(1)}, u32[]{:S(2)}, u32[]{:S(2)}) collective-permute-start(bf16[1024,128]{1,0:T(8,128)(2,1)S(1)} %collective-permute-done.5.refs_3_), channel_id=1, source_target_pairs={{0,8},{8,0},{16,24},{24,16},{32,40},{40,32},{48,56},{56,48},{64,72... | collective-permute-start | bytes 786440 | tf_op jit(solution)/shard_map/ppermute | solution.py:32
  11.6 8.7 %collective-permute-start.7 = (bf16[1024,128]{1,0:T(8,128)(2,1)S(1)}, bf16[1024,128]{1,0:T(8,128)(2,1)S(1)}, u32[]{:S(2)}, u32[]{:S(2)}) collective-permute-start(bf16[1024,128]{1,0:T(8,128)(2,1)S(1)} %collective-permute-done.4.refs_2_), channel_id=1, source_target_pairs={{0,8},{8,0},{16,24},{24,16},{32,40},{40,32},{48,56},{56,48},{64,72... | collective-permute-start | bytes 786440 | tf_op jit(solution)/shard_map/ppermute | solution.py:32
  17.2 3.2 %collective-permute-start.9 = (bf16[1024,128]{1,0:T(8,128)(2,1)S(1)}, bf16[1024,128]{1,0:T(8,128)(2,1)S(1)}, u32[]{:S(2)}, u32[]{:S(2)}) collective-permute-start(bf16[1024,128]{1,0:T(8,128)(2,1)S(1)} %collective-permute-done.3.refs_1_), channel_id=1, source_target_pairs={{0,8},{8,0},{16,24},{24,16},{32,40},{40,32},{48,56},{56,48},{64,72... | collective-permute-start | bytes 786440 | tf_op jit(solution)/shard_map/ppermute | solution.py:32
  17.2 10.7 %collective-permute-start.2 = (bf16[144,1024]{1,0:T(8,128)(2,1)S(1)}, bf16[144,1024]{1,0:T(8,128)(2,1)S(1)}, u32[]{:S(2)}, u32[]{:S(2)}) collective-permute-start(bf16[144,1024]{1,0:T(8,128)(2,1)S(1)} %pad_maximum_fusion.q_ref), channel_id=1, source_target_pairs={{0,192},{8,200},{16,208},{24,216},{32,224},{40,232},{48,240},{56,2... | collective-permute-start | bytes 884744 | tf_op jit(solution)/shard_map/ppermute | solution.py:32
  20.2 9.3 %collective-permute-start.1 = (bf16[144,1024]{1,0:T(8,128)(2,1)S(1)}, bf16[144,1024]{1,0:T(8,128)(2,1)S(1)}, u32[]{:S(2)}, u32[]{:S(2)}) collective-permute-start(bf16[144,1024]{1,0:T(8,128)(2,1)S(1)} %pad_maximum_fusion.q_ref), channel_id=1, source_target_pairs={{0,64},{8,72},{16,80},{24,88},{32,96},{40,104},{48,112},{56,120},{... | collective-permute-start | bytes 884744 | tf_op jit(solution)/shard_map/ppermute | solution.py:32
  24.9 16.1 %collective-permute-start.10 = (bf16[128,1152]{1,0:T(8,128)(2,1)S(1)}, bf16[128,1152]{1,0:T(8,128)(2,1)S(1)}, u32[]{:S(2)}, u32[]{:S(2)}) collective-permute-start(bf16[128,1152]{1,0:T(8,128)(2,1)S(1)} %get-tuple-element.12), channel_id=1, source_target_pairs={{0,128},{8,136},{16,144},{24,152},{32,160},{40,168},{48,176},{56,1... | collective-permute-start | bytes 884744 | tf_op jit(solution)/shard_map/ppermute | solution.py:32
  39.4 8.4 %collective-permute-start.11 = (bf16[128,1152]{1,0:T(8,128)(2,1)S(1)}, bf16[128,1152]{1,0:T(8,128)(2,1)S(1)}, u32[]{:S(2)}, u32[]{:S(2)}) collective-permute-start(bf16[128,1152]{1,0:T(8,128)(2,1)S(1)} %get-tuple-element.13), channel_id=1, source_target_pairs={{0,64},{8,72},{16,80},{24,88},{32,96},{40,104},{48,112},{56,120},{... | collective-permute-start | bytes 884744 | tf_op jit(solution)/shard_map/ppermute | solution.py:32
  39.5 9.6 %collective-permute-start.12 = (bf16[128,1152]{1,0:T(8,128)(2,1)S(1)}, bf16[128,1152]{1,0:T(8,128)(2,1)S(1)}, u32[]{:S(2)}, u32[]{:S(2)}) collective-permute-start(bf16[128,1152]{1,0:T(8,128)(2,1)S(1)} %get-tuple-element.14), channel_id=1, source_target_pairs={{0,192},{8,200},{16,208},{24,216},{32,224},{40,232},{48,240},{56,2... | collective-permute-start | bytes 884744 | tf_op jit(solution)/shard_map/ppermute | solution.py:32
